TPU v7x, 256 devices: a whole 4x4x8 slice. The times are simulated.
256 devices in a mesh: ctx: 16 (over x, y), exp: 16 (over z, core).
Axes of the slice: x: 4, y: 4, z: 8, core: 2. Of those that a mesh axis runs over, the one named last changes fastest.
Arguments:
- inner_input: bfloat16 [2048, 8192], P('ctx', 'exp'), may hold values from -6 to 6
- gate_input: bfloat16 [2048, 8192], P('ctx', 'exp'), may hold values from -6 to 6
- step_codes: int32 [2048, 8192], P('ctx', 'exp'), may hold values from 4 to 16384
- conv_weight: float32 [4, 8192], P(None, 'exp'), may hold values from -3 to 3
- conv_bias: float32 [8192], P('exp'), may hold values from -3 to 3
- decay_rates: float32 [16, 8192], P(None, 'exp')
- skip_gain: float32 [8192], P('exp'), may hold values from 0.5 to 1.5
- state_proj: bfloat16 [8192, 32], P('exp'), may hold values from -0.0625 to 0.0625
- out_proj: bfloat16 [8192, 4096], P('exp'), may hold values from -0.0625 to 0.0625
- residual: bfloat16 [2048, 4096], P(('ctx', 'exp')), may hold values from -6 to 6
- norm_gain: float32 [4096], replicated, may hold values from 0.25 to 1.75
- expert_ids: int32 [2048, 2], P(('ctx', 'exp')), may hold values from 0 to 15, all different within a row; in each aligned block of 8 rows (0 to 7, 8 to 15, ...) at most 2 rows name the same one
- gate_codes: int32 [2048, 2], P(('ctx', 'exp')), may hold values from 1 to 255
- up_weight: bfloat16 [16, 4096, 8192], P('exp', None, 'ctx'), may hold values from -0.09375 to 0.09375
- down_weight: bfloat16 [16, 8192, 4096], P('exp', 'ctx'), may hold values from -0.0625 to 0.0625
Outputs:
- layer_out: bfloat16 [2048, 4096], P(('ctx', 'exp'))
Inputs may be any that keep to these rules, and one draw needn't show every extreme that they name: `expert_ids`: each row names 2 different experts. In each aligned block of 8 rows (the tokens of one device) no expert is named by more than 2 rows.
All inputs are finite; a program needn't handle non-finite values.
Results may differ from a plain program's by a relative error of at most 0.028.
Values may be sent and summed in bfloat16 or wider, within the bound.
No kernel may reach another device: no remote copies, remote signals or barrier semaphores. Data moves between devices by JAX's collectives and lax.ppermute only.
A program may use at most 128 MiB of HBM per device.

v0:
```python
import functools
import math
import jax
import jax.numpy as jnp
from jax import lax
from jax.experimental import pallas as pl
from jax.experimental.pallas import tpu as pltpu
from jax.sharding import PartitionSpec as P

F32 = jnp.float32
BF16 = jnp.bfloat16
SIDE_X, SIDE_Y = 4, 4
DEPTH, CORES = 8, 2
GROUP = 8
VMEM = pl.BlockSpec(memory_space=pltpu.VMEM)
SMEM = pl.BlockSpec(memory_space=pltpu.SMEM)


def shifted(array, axis, by):
    count = lax.axis_size(axis)
    pairs = [(i, i + by) for i in range(count) if 0 <= i + by < count]
    return lax.ppermute(array, axis, pairs)


def along_plane(array, dx, dy):
    pairs = [
        (x * SIDE_Y + y, (x + dx) % SIDE_X * SIDE_Y + (y + dy) % SIDE_Y)
        for x in range(SIDE_X)
        for y in range(SIDE_Y)
    ]
    return lax.ppermute(array, "ctx", pairs)


def along_depth(array, dz, dc):
    pairs = [
        (z * CORES + c, (z + dz) % DEPTH * CORES + (c + dc) % CORES)
        for z in range(DEPTH)
        for c in range(CORES)
    ]
    return lax.ppermute(array, "exp", pairs)


def silu(v):
    return v / (1.0 + jnp.exp(-v))


def prepare_kernel(inner_ref, border_ref, taps_ref, bias_ref, proj_ref, signal_ref, maps_ref, padded):
    length = inner_ref.shape[0]
    count = taps_ref.shape[0]
    padded[0:8, :] = jnp.zeros((8, padded.shape[1]), F32)
    padded[8 - count + 1 : 8, :] = border_ref[...].astype(F32)
    padded[8:, :] = inner_ref[...].astype(F32)
    total = taps_ref[0:1, :] * padded[8 - count + 1 : 8 - count + 1 + length, :]
    for k in range(1, count):
        start = 8 - count + 1 + k
        total = total + taps_ref[k : k + 1, :] * padded[start : start + length, :]
    signal = silu(total + bias_ref[...])
    signal_ref[...] = signal
    maps_ref[...] = lax.dot_general(
        proj_ref[...],
        signal.astype(BF16),
        (((0,), (1,)), ((), ())),
        preferred_element_type=F32,
    )


def recur(maps_ref, codes_ref, signal_ref, rates, state, out_ref):
    width = codes_ref.shape[1]
    count = rates.shape[0]
    tiles = width // 128

    def group(g, state):
        rows = pl.ds(pl.multiple_of(g * GROUP, GROUP), GROUP)
        codes = codes_ref[rows, :].astype(F32)
        drive = jnp.minimum(codes * (1.0 / 256.0), 1.0) * signal_ref[rows, :]
        lanes = maps_ref.shape[1]
        maps = pltpu.roll(maps_ref[...], (lanes - g * GROUP) % lanes, 1)
        outs = []
        for k in range(GROUP):
            into = jnp.broadcast_to(maps[:count, k : k + 1], (count, 128))
            if out_ref is not None:
                out_of = jnp.broadcast_to(maps[count:, k : k + 1], (count, 128))
            pieces = []
            new = []
            for i in range(tiles):
                cols = slice(i * 128, (i + 1) * 128)
                decay = jnp.exp2(codes[k : k + 1, cols] * rates[:, cols])
                now = decay * state[i] + into * drive[k : k + 1, cols]
                new.append(now)
                if out_ref is not None:
                    pieces.append(jnp.sum(out_of * now, axis=0, keepdims=True))
            state = tuple(new)
            if out_ref is not None:
                outs.append(jnp.concatenate(pieces, axis=1))
        if out_ref is not None:
            out_ref[rows, :] = jnp.concatenate(outs, axis=0)
        return state

    return lax.fori_loop(0, codes_ref.shape[0] // GROUP, group, state)


def end_kernel(parts_ref, codes_ref, signal_ref, rates_ref, maps_ref, sent_ref):
    maps = parts_ref[0]
    for i in range(1, parts_ref.shape[0]):
        maps = maps + parts_ref[i]
    maps_ref[...] = maps
    rates = rates_ref[...] * (-math.log2(math.e) / 256.0)
    count, width = rates.shape
    zero = tuple(jnp.zeros((count, 128), F32) for _ in range(width // 128))
    state = jnp.concatenate(recur(maps_ref, codes_ref, signal_ref, rates, zero, None), axis=1)
    total = jnp.sum(codes_ref[...].astype(F32), axis=0, keepdims=True)
    rows = lax.broadcasted_iota(jnp.int32, (count, width), 0)
    packed = jnp.zeros((count, width), F32)
    for i in range(3):
        part = total.astype(BF16).astype(F32)
        packed = jnp.where(rows == i, part, packed)
        total = total - part
    sent_ref[...] = jnp.concatenate([state, packed], axis=0).astype(BF16)


def scan_kernel(
    where_ref, ends_ref, maps_ref, codes_ref, signal_ref, rates_ref, skip_ref, gate_ref, gated_ref, out
):
    rates = rates_ref[...] * (-math.log2(math.e) / 256.0)
    count, width = rates.shape

    def hop(j, state):
        block = ends_ref[j].astype(F32)
        total = block[count : count + 1] + block[count + 1 : count + 2] + block[count + 2 : count + 3]
        return jnp.exp2(total * rates) * state + block[:count]

    start = lax.fori_loop(0, where_ref[0], hop, jnp.zeros((count, width), F32))
    state = tuple(start[:, i * 128 : (i + 1) * 128] for i in range(width // 128))
    recur(maps_ref, codes_ref, signal_ref, rates, state, out)
    z, c = where_ref[1], where_ref[2]

    def gate(j, carry):
        rows = pl.ds(pl.multiple_of(j * GROUP, GROUP), GROUP)
        to = (j % CORES + CORES - c) % CORES * DEPTH + (j // CORES + DEPTH - z) % DEPTH
        value = out[rows, :] + skip_ref[...] * signal_ref[rows, :]
        gated_ref[pl.ds(pl.multiple_of(to * GROUP, GROUP), GROUP), :] = value * silu(
            gate_ref[rows, :].astype(F32)
        )
        return carry

    lax.fori_loop(0, codes_ref.shape[0] // GROUP, gate, 0)


def state_space(inner_input, gate_input, step_codes, conv_weight, conv_bias, decay_rates, skip_gain, state_proj):
    length, width = inner_input.shape
    taps = conv_weight.shape[0]
    count = decay_rates.shape[0]
    border = shifted(inner_input[length - taps + 1 :], "ctx", 1)
    signal, part = pl.pallas_call(
        prepare_kernel,
        out_shape=(
            jax.ShapeDtypeStruct((length, width), F32),
            jax.ShapeDtypeStruct((2 * count, length), F32),
        ),
        in_specs=[VMEM] * 5,
        out_specs=(VMEM, VMEM),
        scratch_shapes=[pltpu.VMEM((length + 8, width), F32)],
        name="prepare",
    )(inner_input, border, conv_weight, conv_bias[None], state_proj)
    parts = lax.all_gather(part, "exp")
    maps, sent = pl.pallas_call(
        end_kernel,
        out_shape=(
            jax.ShapeDtypeStruct((2 * count, length), F32),
            jax.ShapeDtypeStruct((2 * count, width), BF16),
        ),
        in_specs=[VMEM] * 4,
        out_specs=(VMEM, VMEM),
        name="end_state",
    )(parts, step_codes, signal, decay_rates)
    ends = lax.all_gather(sent, "ctx")
    exp = lax.axis_index("exp")
    where = jnp.stack([lax.axis_index("ctx"), exp // CORES, exp % CORES]).astype(jnp.int32)
    return pl.pallas_call(
        scan_kernel,
        out_shape=jax.ShapeDtypeStruct((length, width), F32),
        in_specs=[SMEM] + [VMEM] * 7,
        out_specs=VMEM,
        scratch_shapes=[pltpu.VMEM((length, width), F32)],
        name="scan",
    )(where, ends, maps, step_codes, signal, decay_rates, skip_gain[None], gate_input)


def project_out(gated, out_proj):
    half = gated.shape[0] // CORES

    def product(rows):
        return jnp.dot(rows.astype(BF16), out_proj, preferred_element_type=F32).astype(BF16)

    theirs = along_depth(product(gated[half:]), 0, 1)
    pair = (product(gated[:half]).astype(F32) + theirs.astype(F32)).astype(BF16)
    blocks = pair.reshape(DEPTH, GROUP, -1)
    total = blocks[0].astype(F32)
    for dz in range(1, DEPTH):
        total = total + along_depth(blocks[dz], dz, 0).astype(F32)
    return total


def sum_side(blocks, dx, dy):
    half = blocks[2].shape[0] // 2
    up = along_plane(blocks[2][:half], dx, dy).astype(F32)
    down = along_plane(blocks[2][half:], -dx, -dy).astype(F32)
    one, three = blocks[1].astype(F32), blocks[3].astype(F32)
    one = jnp.concatenate([one[:half] + up, one[half:]]).astype(BF16)
    three = jnp.concatenate([three[:half], three[half:] + down]).astype(BF16)
    one = along_plane(one, dx, dy)
    three = along_plane(three, -dx, -dy)
    return (blocks[0].astype(F32) + one.astype(F32) + three.astype(F32)).astype(BF16)


def shards(
    inner_input,
    gate_input,
    step_codes,
    conv_weight,
    conv_bias,
    decay_rates,
    skip_gain,
    state_proj,
    out_proj,
    residual,
    norm_gain,
    expert_ids,
    gate_codes,
    up_weight,
    down_weight,
):
    gated = state_space(
        inner_input, gate_input, step_codes, conv_weight, conv_bias, decay_rates, skip_gain, state_proj
    )
    row_count = residual.shape[0]
    mamba_out = project_out(gated, out_proj)
    stream = (residual.astype(F32) + mamba_out).astype(BF16)
    stream_wide = stream.astype(F32)
    normed = (
        stream_wide
        * lax.rsqrt(jnp.mean(stream_wide * stream_wide, axis=-1, keepdims=True) + 1e-05)
        * norm_gain
    ).astype(BF16)
    experts = lax.axis_size("exp") * up_weight.shape[0]
    top_count = expert_ids.shape[1]
    capacity = max(2, 4 * row_count // experts)
    onehot = (
        (expert_ids[:, :, None] == jnp.arange(experts)[None, None, :])
        .astype(jnp.int32)
        .reshape(row_count * top_count, experts)
    )
    before = jnp.cumsum(onehot, axis=0) - onehot
    ranking = jnp.sum(before * onehot, axis=1).reshape(row_count, top_count)
    slot_index = expert_ids * capacity + ranking
    slots = slot_index[:, :, None] == jnp.arange(experts * capacity)[None, None, :]
    dispatch_table = jnp.any(slots, axis=1).astype(BF16)
    up_local = up_weight[0]
    down_local = down_weight[0]
    outgoing = lax.dot_general(
        dispatch_table, normed, (((0,), (0,)), ((), ())), preferred_element_type=F32
    ).astype(BF16)
    arrived = lax.all_to_all(outgoing, "exp", split_axis=0, concat_axis=0, tiled=True)
    segment = lax.all_gather(arrived, "ctx", axis=0, tiled=True)
    hidden = jax.nn.silu(jnp.dot(segment, up_local, preferred_element_type=F32)).astype(BF16)
    partial = jnp.dot(hidden, down_local, preferred_element_type=F32).astype(BF16)
    expert_out = lax.psum_scatter(partial, "ctx", scatter_dimension=0, tiled=True)
    returned = lax.all_to_all(expert_out, "exp", split_axis=0, concat_axis=0, tiled=True)
    gate_weights = gate_codes.astype(F32)
    gate_weights = gate_weights / jnp.sum(gate_weights, axis=1, keepdims=True)
    picked = jnp.take(returned, slot_index, axis=0).astype(F32)
    mixture_out = jnp.sum(gate_weights[:, :, None] * picked, axis=1)
    return (stream_wide + mixture_out).astype(BF16)


def solution(mesh):
    return jax.shard_map(
        shards,
        mesh=mesh,
        in_specs=(
            P("ctx", "exp"),
            P("ctx", "exp"),
            P("ctx", "exp"),
            P(None, "exp"),
            P("exp"),
            P(None, "exp"),
            P("exp"),
            P("exp", None),
            P("exp", None),
            P(("ctx", "exp"), None),
            P(),
            P(("ctx", "exp"), None),
            P(("ctx", "exp"), None),
            P("exp", None, "ctx"),
            P("exp", "ctx", None),
        ),
        out_specs=P(("ctx", "exp"), None),
        check_vma=False,
    )
```

profile of v0, /device:TPU:1, one launch (start us, length us, event | category | flops | bytes accessed | tf_op | source)
XLA Modules:
  0.0 298.2 jit_solution(10387768633947795023)
XLA Ops:
  6.5 0.7 slice.43
  7.2 4.0 %collective-permute-start = (bf16[3,512]{1,0:T(4,128)(2,1)S(1)}, bf16[3,512]{1,0:T(4,128)(2,1)S(1)}, u32[]{:S(2)}, u32[]{:S(2)}) collective-permute-start(bf16[3,512]{1,0:T(4,128)(2,1)S(1)} %slice.43), channel_id=1, source_target_pairs={{0,16},{16,32},{32,48},{48,64},{64,80},{80,96},{96,112},{112,128},... | collective-permute-start | bytes 9224 | tf_op jit(solution)/shard_map/ppermute | solution.py:22
  11.3 0.6 pad_add_fusion.where_ref
  11.9 1.5 copy.24.proj_ref
  13.4 0.0 collective-permute-done.border_ref
  13.4 0.6 copy-done.2
  14.0 2.0 prepare.1
  16.0 23.2 %all-gather = f32[512,128]{1,0:T(8,128)} all-gather(f32[32,128]{1,0:T(8,128)} %get-tuple-element.9), channel_id=2, replica_groups=mesh['ctx'=16,'exp'=16] {'exp'}, dimensions={0}, use_global_device_ids=true | all-gather | bytes 278528 | tf_op jit(solution)/shard_map/all_gather | solution.py:165
  39.2 4.6 %end_state.1 = (f32[32,128]{1,0:T(8,128)}, bf16[32,512]{1,0:T(8,128)(2,1)}) custom-call(f32[16,32,128]{2,1,0:T(8,128)} %bitcast.21, s32[128,512]{1,0:T(8,128)} %codes_ref.3, f32[128,512]{1,0:T(8,128)} %get-tuple-element.10.signal_ref, f32[16,512]{1,0:T(8,128)} %rates_ref.3), custom_call_target="tpu_custom_call" | custom-call | tf_op jit(solution)/shard_map/end_state/pallas_call | solution.py:166
  43.8 22.4 %all-gather.1 = bf16[512,512]{1,0:T(8,128)(2,1)} all-gather(bf16[32,512]{1,0:T(8,128)(2,1)} %get-tuple-element.11), channel_id=3, replica_groups=mesh['ctx'=16,'exp'=16] {'ctx'}, dimensions={0}, use_global_device_ids=true | all-gather | bytes 557056 | tf_op jit(solution)/shard_map/all_gather | solution.py:176
  66.2 6.0 %scan.1 = f32[128,512]{1,0:T(8,128)} custom-call(s32[3]{0:T(128)} %pad_add_fusion.where_ref, bf16[16,32,512]{2,1,0:T(8,128)(2,1)} %bitcast.20, f32[32,128]{1,0:T(8,128)} %get-tuple-element.12.maps_ref, s32[128,512]{1,0:T(8,128)} %codes_ref.3, f32[128,512]{1,0:T(8,128)} %get-tuple-element.10.signal_ref, f32[16,512]{1,0:T(8,128)} %rates_ref.3, ...), custom_call_target="tpu_custom_call" | custom-call | tf_op jit(solution)/shard_map/scan/pallas_call | solution.py:179
  72.2 1.0 convert.4
  73.2 3.0 %convolution_convert_fusion.1 = bf16[64,4096]{1,0:T(8,128)(2,1)S(1)} fusion(bf16[512,4096]{1,0:T(8,128)(2,1)} %param.23, bf16[128,512]{1,0:T(8,128)(2,1)S(1)} %convert.4), kind=kOutput, calls=%fused_computation.2 | convolution fusion | flops 268697600 | bytes 4784128 | tf_op jit(solution)/shard_map/dot_general | solution.py:193
  76.2 0.0 copy-start
  76.2 0.0 copy-start.1
  76.2 5.5 %collective-permute-start.1 = (bf16[64,4096]{1,0:T(8,128)(2,1)S(1)}, bf16[64,4096]{1,0:T(8,128)(2,1)S(1)}, u32[]{:S(2)}, u32[]{:S(2)}) collective-permute-start(bf16[64,4096]{1,0:T(8,128)(2,1)S(1)} %convolution_convert_fusion.1), channel_id=1, source_target_pairs={{0,1},{1,0},{2,3},{3,2},{4,5},{5,4},{6,7},{7,6},{8,9},{9,8},{10,11... | collective-permute-start | bytes 1572872 | tf_op jit(solution)/shard_map/ppermute | solution.py:40
  81.7 0.0 copy-done.3
  81.7 0.1 copy.26
  81.8 0.1 eq.31
  81.9 0.1 fusion.17
  82.0 0.2 select_reduce_fusion
  82.2 0.1 reshape.45
  82.2 1.0 collective-permute-done.1
  83.2 3.0 %add_convert_fusion = bf16[64,4096]{1,0:T(8,128)(2,1)S(1)} fusion(bf16[64,4096]{1,0:T(8,128)(2,1)S(1)} %collective-permute-done.1, bf16[512,4096]{1,0:T(8,128)(2,1)} %param.23, bf16[128,512]{1,0:T(8,128)(2,1)S(1)} %convert.4), kind=kOutput, calls=%fused_computation.10 | convolution fusion | flops 269746176 | bytes 5308416 | tf_op jit(solution)/shard_map/dot_general | solution.py:193
  86.3 0.1 collective-permute-start.2
  86.4 0.6 collective-permute-start.3
  87.1 0.1 copy.28
  87.2 2.2 collective-permute-start.4
  89.4 2.8 collective-permute-start.5
  92.2 1.6 collective-permute-start.6
  93.8 0.0 collective-permute-done.2
  93.8 3.6 %collective-permute-start.7 = (bf16[8,4096]{1,0:T(8,128)(2,1)S(1)}, bf16[8,4096]{1,0:T(8,128)(2,1)S(1)}, u32[]{:S(2)}, u32[]{:S(2)}) collective-permute-start(bf16[8,4096]{1,0:T(8,128)(2,1)S(1)} %get-tuple-element.19), channel_id=1, source_target_pairs={{0,12},{1,13},{2,14},{3,15},{4,0},{5,1},{6,2},{7,3},{8,4},{9,5},{1... | collective-permute-start | bytes 196616 | tf_op jit(solution)/shard_map/ppermute | solution.py:40
  97.3 0.0 collective-permute-done.3
  97.3 0.8 collective-permute-start.8
  98.1 0.1 fusion.18
  98.2 1.3 collective-permute-done.4
  99.5 0.1 collective-permute-done.5
  99.6 0.2 collective-permute-done.6
  99.7 5.8 %collective-permute-done.7 = bf16[8,4096]{1,0:T(8,128)(2,1)S(1)} collective-permute-done((bf16[8,4096]{1,0:T(8,128)(2,1)S(1)}, bf16[8,4096]{1,0:T(8,128)(2,1)S(1)}, u32[]{:S(2)}, u32[]{:S(2)}) %collective-permute-start.7) | collective-permute-done | bytes 65568 | tf_op jit(solution)/shard_map/ppermute | solution.py:40
  105.5 0.2 collective-permute-done.8
  105.8 0.2 fusion.6
  106.0 0.3 convolution_convert_fusion.3
  106.3 0.2 all_to_all.16
  106.5 17.1 %all_to_all.24 = bf16[16,2,4096]{2,1,0:T(2,128)(2,1)S(1)} all-to-all(bf16[16,2,4096]{2,1,0:T(2,128)(2,1)S(1)} %all_to_all.16), channel_id=1, replica_groups=mesh['ctx'=16,'exp'=16] {'exp'}, dimensions={0} | all-to-all | bytes 524288 | tf_op jit(solution)/shard_map/all_to_all | solution.py:263
  123.6 0.8 all_to_all.18
  124.4 0.0 all-gather.4.cloned.1.call-update
  124.4 0.2 reduce-scatter.2.cloned.1.call-start
  124.6 50.6 %all-gather.4.cloned.1.call-done = bf16[512,4096]{1,0:T(8,128)(2,1)} async-done(((bf16[32,4096]{1,0:T(8,128)(2,1)}), bf16[512,4096]{1,0:T(8,128)(2,1)}) %all-gather.4.cloned.1.call-update) | async-done | bytes 4194320 | tf_op jit(solution)/shard_map/all_gather | solution.py:264
  175.2 6.1 %multiply_convert_fusion = bf16[512,512]{1,0:T(8,128)(2,1)S(1)} fusion(bf16[512,4096]{1,0:T(8,128)(2,1)} %all-gather.4.cloned.1.call-done, bf16[1,4096,512]{2,1,0:T(8,128)(2,1)} %param.28), kind=kOutput, calls=%fused_computation.9 | convolution fusion | flops 2148794368 | bytes 8912896 | tf_op jit(solution)/shard_map/dot_general | solution.py:265
  181.3 0.0 copy-done.5
  181.3 4.3 %convolution_convert_fusion = bf16[512,4096]{1,0:T(8,128)(2,1)} fusion(bf16[512,512]{1,0:T(8,128)(2,1)S(1)} %multiply_convert_fusion, bf16[1,512,4096]{2,1,0:T(8,128)(2,1)S(1)} %copy-done.5), kind=kOutput, calls=%fused_computation.1 | convolution fusion | flops 2149580800 | bytes 8912896 | tf_op jit(solution)/shard_map/dot_general | solution.py:266
  185.6 0.0 reduce-scatter.2.cloned.1.call-update
  185.6 80.9 %reduce-scatter.2.cloned.1.call-done = bf16[32,4096]{1,0:T(8,128)(2,1)} async-done(((bf16[512,4096]{1,0:T(8,128)(2,1)}), bf16[32,4096]{1,0:T(8,128)(2,1)}) %reduce-scatter.2.cloned.1.call-update) | async-done | bytes 262160 | tf_op jit(solution)/shard_map/reduce_scatter | solution.py:267
  266.5 1.8 all_to_all.19
  268.3 9.4 %all-to-all-start.1 = ((bf16[16,2,4096]{2,1,0:T(2,128)(2,1)}), bf16[16,2,4096]{2,1,0:T(2,128)(2,1)S(1)}, u32[]{:S(2)}, u32[]{:S(2)}) async-start(bf16[16,2,4096]{2,1,0:T(2,128)(2,1)} %all_to_all.19), calls=%async_computation.2 | async-start | bytes 524288 | tf_op jit(solution)/shard_map/all_to_all | solution.py:268
  277.7 0.1 reshape.48
  277.8 0.0 copy-done.4
  277.8 0.1 copy.25
  277.9 11.5 %all-to-all-done.1 = bf16[16,2,4096]{2,1,0:T(2,128)(2,1)S(1)} async-done(((bf16[16,2,4096]{2,1,0:T(2,128)(2,1)}), bf16[16,2,4096]{2,1,0:T(2,128)(2,1)S(1)}, u32[]{:S(2)}, u32[]{:S(2)}) %all-to-all-start.1) | async-done | bytes 262176 | tf_op jit(solution)/shard_map/all_to_all | solution.py:268
  289.4 0.1 all_to_all.21
  289.5 0.6 gather_fusion
  290.2 0.1 reshape.47
  290.3 0.5 multiply_reduce_fusion
  290.7 0.6 fusion.9
  (15 shorter events, 0.1 us)
Async XLA Ops:
  6.5 168.7 %all-gather.4.cloned.1.call-start = ((), (), s32[]{:S(2)}) async-start(), calls=%async_computation.3 | async-start | bytes 4456448 | tf_op jit(solution)/shard_map/all_gather | solution.py:264
  7.2 6.2 %collective-permute-start = (bf16[3,512]{1,0:T(4,128)(2,1)S(1)}, bf16[3,512]{1,0:T(4,128)(2,1)S(1)}, u32[]{:S(2)}, u32[]{:S(2)}) collective-permute-start(bf16[3,512]{1,0:T(4,128)(2,1)S(1)} %slice.43), channel_id=1, source_target_pairs={{0,16},{16,32},{32,48},{48,64},{64,80},{80,96},{96,112},{112,128},... | collective-permute-start | bytes 9224 | tf_op jit(solution)/shard_map/ppermute | solution.py:22
  13.4 0.6 copy-start.2
  16.0 65.7 %copy-start.3 = (s32[8,2]{0,1:T(2,128)S(1)}, s32[8,2]{0,1:T(2,128)}, u32[]{:S(2)}) copy-start(s32[8,2]{0,1:T(2,128)} %param.26) | copy-start | bytes 196
  76.2 29.6 %copy-start = (bf16[8,4096]{1,0:T(8,128)(2,1)S(1)}, bf16[8,4096]{1,0:T(8,128)(2,1)}, u32[]{:S(2)}) copy-start(bf16[8,4096]{1,0:T(8,128)(2,1)} %param.24) | copy-start | bytes 196612
  76.2 29.8 %copy-start.1 = (f32[4096]{0:T(1024)S(1)}, f32[4096]{0:T(1024)}, u32[]{:S(2)}) copy-start(f32[4096]{0:T(1024)} %param.25) | copy-start | bytes 49156
  76.2 7.0 %collective-permute-start.1 = (bf16[64,4096]{1,0:T(8,128)(2,1)S(1)}, bf16[64,4096]{1,0:T(8,128)(2,1)S(1)}, u32[]{:S(2)}, u32[]{:S(2)}) collective-permute-start(bf16[64,4096]{1,0:T(8,128)(2,1)S(1)} %convolution_convert_fusion.1), channel_id=1, source_target_pairs={{0,1},{1,0},{2,3},{3,2},{4,5},{5,4},{6,7},{7,6},{8,9},{9,8},{10,11... | collective-permute-start | bytes 1572872 | tf_op jit(solution)/shard_map/ppermute | solution.py:40
  86.3 7.4 %collective-permute-start.2 = (bf16[8,4096]{1,0:T(8,128)(2,1)S(1)}, bf16[8,4096]{1,0:T(8,128)(2,1)S(1)}, u32[]{:S(2)}, u32[]{:S(2)}) collective-permute-start(bf16[8,4096]{1,0:T(8,128)(2,1)S(1)} %get-tuple-element.17), channel_id=1, source_target_pairs={{0,2},{1,3},{2,4},{3,5},{4,6},{5,7},{6,8},{7,9},{8,10},{9,11},{10,... | collective-permute-start | bytes 196616 | tf_op jit(solution)/shard_map/ppermute | solution.py:40
  86.4 10.9 %collective-permute-start.3 = (bf16[8,4096]{1,0:T(8,128)(2,1)S(1)}, bf16[8,4096]{1,0:T(8,128)(2,1)S(1)}, u32[]{:S(2)}, u32[]{:S(2)}) collective-permute-start(bf16[8,4096]{1,0:T(8,128)(2,1)S(1)} %get-tuple-element.23), channel_id=1, source_target_pairs={{0,4},{1,5},{2,6},{3,7},{4,8},{5,9},{6,10},{7,11},{8,12},{9,13},{1... | collective-permute-start | bytes 196616 | tf_op jit(solution)/shard_map/ppermute | solution.py:40
  87.2 12.3 %collective-permute-start.4 = (bf16[8,4096]{1,0:T(8,128)(2,1)S(1)}, bf16[8,4096]{1,0:T(8,128)(2,1)S(1)}, u32[]{:S(2)}, u32[]{:S(2)}) collective-permute-start(bf16[8,4096]{1,0:T(8,128)(2,1)S(1)} %get-tuple-element.22), channel_id=1, source_target_pairs={{0,6},{1,7},{2,8},{3,9},{4,10},{5,11},{6,12},{7,13},{8,14},{9,15},... | collective-permute-start | bytes 196616 | tf_op jit(solution)/shard_map/ppermute | solution.py:40
  89.4 10.2 %collective-permute-start.5 = (bf16[8,4096]{1,0:T(8,128)(2,1)S(1)}, bf16[8,4096]{1,0:T(8,128)(2,1)S(1)}, u32[]{:S(2)}, u32[]{:S(2)}) collective-permute-start(bf16[8,4096]{1,0:T(8,128)(2,1)S(1)} %get-tuple-element.21), channel_id=1, source_target_pairs={{0,8},{1,9},{2,10},{3,11},{4,12},{5,13},{6,14},{7,15},{8,0},{9,1},... | collective-permute-start | bytes 196616 | tf_op jit(solution)/shard_map/ppermute | solution.py:40
  92.2 7.6 %collective-permute-start.6 = (bf16[8,4096]{1,0:T(8,128)(2,1)S(1)}, bf16[8,4096]{1,0:T(8,128)(2,1)S(1)}, u32[]{:S(2)}, u32[]{:S(2)}) collective-permute-start(bf16[8,4096]{1,0:T(8,128)(2,1)S(1)} %get-tuple-element.20), channel_id=1, source_target_pairs={{0,10},{1,11},{2,12},{3,13},{4,14},{5,15},{6,0},{7,1},{8,2},{9,3},... | collective-permute-start | bytes 196616 | tf_op jit(solution)/shard_map/ppermute | solution.py:40
  93.8 11.8 %collective-permute-start.7 = (bf16[8,4096]{1,0:T(8,128)(2,1)S(1)}, bf16[8,4096]{1,0:T(8,128)(2,1)S(1)}, u32[]{:S(2)}, u32[]{:S(2)}) collective-permute-start(bf16[8,4096]{1,0:T(8,128)(2,1)S(1)} %get-tuple-element.19), channel_id=1, source_target_pairs={{0,12},{1,13},{2,14},{3,15},{4,0},{5,1},{6,2},{7,3},{8,4},{9,5},{1... | collective-permute-start | bytes 196616 | tf_op jit(solution)/shard_map/ppermute | solution.py:40
  97.3 8.4 %collective-permute-start.8 = (bf16[8,4096]{1,0:T(8,128)(2,1)S(1)}, bf16[8,4096]{1,0:T(8,128)(2,1)S(1)}, u32[]{:S(2)}, u32[]{:S(2)}) collective-permute-start(bf16[8,4096]{1,0:T(8,128)(2,1)S(1)} %get-tuple-element.18), channel_id=1, source_target_pairs={{0,14},{1,15},{2,0},{3,1},{4,2},{5,3},{6,4},{7,5},{8,6},{9,7},{10,... | collective-permute-start | bytes 196616 | tf_op jit(solution)/shard_map/ppermute | solution.py:40
  124.4 142.1 %reduce-scatter.2.cloned.1.call-start = ((), (), s32[]{:S(2)}) async-start(), calls=%async_computation.4 | async-start | bytes 4456448 | tf_op jit(solution)/shard_map/reduce_scatter | solution.py:267
  175.2 6.1 %copy-start.5 = (bf16[1,512,4096]{2,1,0:T(8,128)(2,1)S(1)}, bf16[1,512,4096]{2,1,0:T(8,128)(2,1)}, u32[]{:S(2)}) copy-start(bf16[1,512,4096]{2,1,0:T(8,128)(2,1)} %param.29) | copy-start | bytes 12582916
  185.6 92.2 %copy-start.4 = (s32[8,2]{0,1:T(2,128)S(1)}, s32[8,2]{0,1:T(2,128)}, u32[]{:S(2)}) copy-start(s32[8,2]{0,1:T(2,128)} %param.27) | copy-start | bytes 196
  268.3 21.1 %all-to-all-start.1 = ((bf16[16,2,4096]{2,1,0:T(2,128)(2,1)}), bf16[16,2,4096]{2,1,0:T(2,128)(2,1)S(1)}, u32[]{:S(2)}, u32[]{:S(2)}) async-start(bf16[16,2,4096]{2,1,0:T(2,128)(2,1)} %all_to_all.19), calls=%async_computation.2 | async-start | bytes 524288 | tf_op jit(solution)/shard_map/all_to_all | solution.py:268
Sparse Core Ops, SparseCore 0:
  124.5 50.6 all-gather.3
  185.7 80.7 reduce-scatter.1
where the time goes:
time: 299 us; the launch traced here: 298 us
  waiting for transfers between devices  152 us (51%)
  blocking collectives  62.7 us (21%)
  starting transfers between devices  30.8 us (10%)
  matrix products  16.7 us (6%)
  between operations  13.6 us (5%)
  Pallas kernels  12.6 us (4%)
  local copies, waits for them, and re-layouts  6.99 us (2%)
  other arithmetic  3.3 us (1%)
    reduce_scatter x1, waiting for transfers between devices, shards(): lax.psum_scatter(partial, 'ctx', scatter_dimension=0, tiled=True)  80.9 us
    all_gather x1, waiting for transfers between devices, shards(): segment = lax.all_gather(arrived, 'ctx', axis=0, tiled=True)  50.6 us
    all_gather x1, blocking collectives, state_space(): parts = lax.all_gather(part, 'exp')  23.2 us
    all_gather x1, blocking collectives, state_space(): ends = lax.all_gather(sent, 'ctx')  22.4 us
    ppermute x8, starting transfers between devices, along_depth(): return lax.ppermute(array, 'exp', pairs)  17.1 us
    all_to_all x1, blocking collectives, shards(): lax.all_to_all(outgoing, 'exp', split_axis=0, concat_axis=0, tiled=True)  17.1 us
    all_to_all x1, waiting for transfers between devices, shards(): lax.all_to_all(expert_out, 'exp', split_axis=0, concat_axis=0, tiled=True)  11.5 us
    all_to_all x1, starting transfers between devices, shards(): lax.all_to_all(expert_out, 'exp', split_axis=0, concat_axis=0, tiled=True)  9.38 us
  transfers between devices with their start and end apart: 12, of which 9 were waited for; matrix products, arithmetic and copies ran while one was open for 1% of the time, Pallas kernels for 0%

commit v1 on v0

--- a/solution.py
+++ b/solution.py
@@ -31,13 +31,25 @@
     return lax.ppermute(array, "ctx", pairs)
 
 
-def along_depth(array, dz, dc):
-    pairs = [
-        (z * CORES + c, (z + dz) % DEPTH * CORES + (c + dc) % CORES)
-        for z in range(DEPTH)
-        for c in range(CORES)
+def along_depth(array, target):
+    pairs = []
+    for z in range(DEPTH):
+        for c in range(CORES):
+            to_z, to_c = target(z, c)
+            pairs.append((z * CORES + c, to_z % DEPTH * CORES + to_c))
+    return lax.ppermute(array, "exp", pairs)
+
+
+def near(array):
+    return [
+        along_depth(array, lambda z, c: (z, 1 - c)),
+        along_depth(array, lambda z, c: (z ^ 1, c)),
+        along_depth(array, lambda z, c: (z ^ 1, 1 - c)),
     ]
-    return lax.ppermute(array, "exp", pairs)
+
+
+def far(arrays):
+    return [along_depth(a, lambda z, c, k=k: (z + 2 * k, c)) for k, a in enumerate(arrays) if k]
 
 
 def silu(v):
@@ -59,7 +71,7 @@
     maps_ref[...] = lax.dot_general(
         proj_ref[...],
         signal.astype(BF16),
-        (((0,), (1,)), ((), ())),
+        (((1,), (1,)), ((), ())),
         preferred_element_type=F32,
     )
 
@@ -99,11 +111,8 @@
     return lax.fori_loop(0, codes_ref.shape[0] // GROUP, group, state)
 
 
-def end_kernel(parts_ref, codes_ref, signal_ref, rates_ref, maps_ref, sent_ref):
-    maps = parts_ref[0]
-    for i in range(1, parts_ref.shape[0]):
-        maps = maps + parts_ref[i]
-    maps_ref[...] = maps
+def end_kernel(a_ref, b_ref, c_ref, d_ref, codes_ref, signal_ref, rates_ref, maps_ref, sent_ref):
+    maps_ref[...] = (a_ref[...] + b_ref[...]) + (c_ref[...] + d_ref[...])
     rates = rates_ref[...] * (-math.log2(math.e) / 256.0)
     count, width = rates.shape
     zero = tuple(jnp.zeros((count, 128), F32) for _ in range(width // 128))
@@ -119,13 +128,16 @@
 
 
 def scan_kernel(
-    where_ref, ends_ref, maps_ref, codes_ref, signal_ref, rates_ref, skip_ref, gate_ref, gated_ref, out
+    where_ref, ends_ref, maps_ref, codes_ref, signal_ref, rates_ref, skip_ref, gate_ref, gated_ref, out, arranged
 ):
     rates = rates_ref[...] * (-math.log2(math.e) / 256.0)
     count, width = rates.shape
 
+    x, y = where_ref[0] // SIDE_Y, where_ref[0] % SIDE_Y
+
     def hop(j, state):
-        block = ends_ref[j].astype(F32)
+        at = (x + SIDE_X - j // SIDE_Y) % SIDE_X * SIDE_Y + (y + SIDE_Y - j % SIDE_Y) % SIDE_Y
+        block = ends_ref[pl.ds(pl.multiple_of(at * 2 * count, 2 * count), 2 * count), :].astype(F32)
         total = block[count : count + 1] + block[count + 1 : count + 2] + block[count + 2 : count + 3]
         return jnp.exp2(total * rates) * state + block[:count]
 
@@ -133,17 +145,20 @@
     state = tuple(start[:, i * 128 : (i + 1) * 128] for i in range(width // 128))
     recur(maps_ref, codes_ref, signal_ref, rates, state, out)
     z, c = where_ref[1], where_ref[2]
+    pairs = DEPTH // 2
 
     def gate(j, carry):
         rows = pl.ds(pl.multiple_of(j * GROUP, GROUP), GROUP)
-        to = (j % CORES + CORES - c) % CORES * DEPTH + (j // CORES + DEPTH - z) % DEPTH
+        to_z, to_c = j // CORES, j % CORES
+        to = ((to_c + c) % 2 * 2 + (to_z + z) % 2) * pairs + (to_z // 2 + pairs - z // 2) % pairs
         value = out[rows, :] + skip_ref[...] * signal_ref[rows, :]
-        gated_ref[pl.ds(pl.multiple_of(to * GROUP, GROUP), GROUP), :] = value * silu(
+        arranged[pl.ds(pl.multiple_of(to * GROUP, GROUP), GROUP), :] = value * silu(
             gate_ref[rows, :].astype(F32)
         )
         return carry
 
     lax.fori_loop(0, codes_ref.shape[0] // GROUP, gate, 0)
+    gated_ref[...] = arranged[...].astype(BF16)
 
 
 def state_space(inner_input, gate_input, step_codes, conv_weight, conv_bias, decay_rates, skip_gain, state_proj):
@@ -161,56 +176,90 @@
         out_specs=(VMEM, VMEM),
         scratch_shapes=[pltpu.VMEM((length + 8, width), F32)],
         name="prepare",
-    )(inner_input, border, conv_weight, conv_bias[None], state_proj)
-    parts = lax.all_gather(part, "exp")
+    )(inner_input, border, conv_weight, conv_bias[None], state_proj.T)
+    part = sum(near(part), part)
     maps, sent = pl.pallas_call(
         end_kernel,
         out_shape=(
             jax.ShapeDtypeStruct((2 * count, length), F32),
             jax.ShapeDtypeStruct((2 * count, width), BF16),
         ),
-        in_specs=[VMEM] * 4,
+        in_specs=[VMEM] * 7,
         out_specs=(VMEM, VMEM),
         name="end_state",
-    )(parts, step_codes, signal, decay_rates)
-    ends = lax.all_gather(sent, "ctx")
+    )(part, *far([part] * (DEPTH // 2)), step_codes, signal, decay_rates)
+    ends = jnp.concatenate([sent] + [along_plane(sent, 0, k) for k in range(1, SIDE_Y)])
+    ends = jnp.concatenate([ends] + [along_plane(ends, k, 0) for k in range(1, SIDE_X)])
     exp = lax.axis_index("exp")
     where = jnp.stack([lax.axis_index("ctx"), exp // CORES, exp % CORES]).astype(jnp.int32)
     return pl.pallas_call(
         scan_kernel,
-        out_shape=jax.ShapeDtypeStruct((length, width), F32),
+        out_shape=jax.ShapeDtypeStruct((length, width), BF16),
         in_specs=[SMEM] + [VMEM] * 7,
         out_specs=VMEM,
-        scratch_shapes=[pltpu.VMEM((length, width), F32)],
+        scratch_shapes=[pltpu.VMEM((length, width), F32)] * 2,
         name="scan",
     )(where, ends, maps, step_codes, signal, decay_rates, skip_gain[None], gate_input)
 
 
+def added(*arrays):
+    return sum(a.astype(F32) for a in arrays).astype(BF16)
+
+
 def project_out(gated, out_proj):
-    half = gated.shape[0] // CORES
-
-    def product(rows):
-        return jnp.dot(rows.astype(BF16), out_proj, preferred_element_type=F32).astype(BF16)
-
-    theirs = along_depth(product(gated[half:]), 0, 1)
-    pair = (product(gated[:half]).astype(F32) + theirs.astype(F32)).astype(BF16)
-    blocks = pair.reshape(DEPTH, GROUP, -1)
-    total = blocks[0].astype(F32)
-    for dz in range(1, DEPTH):
-        total = total + along_depth(blocks[dz], dz, 0).astype(F32)
-    return total
-
-
-def sum_side(blocks, dx, dy):
-    half = blocks[2].shape[0] // 2
-    up = along_plane(blocks[2][:half], dx, dy).astype(F32)
-    down = along_plane(blocks[2][half:], -dx, -dy).astype(F32)
-    one, three = blocks[1].astype(F32), blocks[3].astype(F32)
-    one = jnp.concatenate([one[:half] + up, one[half:]]).astype(BF16)
-    three = jnp.concatenate([three[:half], three[half:] + down]).astype(BF16)
-    one = along_plane(one, dx, dy)
-    three = along_plane(three, -dx, -dy)
-    return (blocks[0].astype(F32) + one.astype(F32) + three.astype(F32)).astype(BF16)
+    product = jnp.dot(gated, out_proj, preferred_element_type=F32).astype(BF16)
+    half = product.shape[0] // 2
+    pair = added(product[:half], along_depth(product[half:], lambda z, c: (z, 1 - c)))
+    half = half // 2
+    chip = added(pair[:half], along_depth(pair[half:], lambda z, c: (z ^ 1, c)))
+    blocks = [chip[k * GROUP : (k + 1) * GROUP] for k in range(DEPTH // 2)]
+    return sum((a.astype(F32) for a in far(blocks)), blocks[0].astype(F32))
+
+
+def expert(rows, up, down):
+    hidden = jax.nn.silu(jnp.dot(rows, up, preferred_element_type=F32)).astype(BF16)
+    return jnp.dot(hidden, down, preferred_element_type=F32).astype(BF16)
+
+
+def split(array, parts):
+    size = array.shape[0] // parts
+    return [array[k * size : (k + 1) * size] for k in range(parts)]
+
+
+def run_expert(arrived, up, down):
+    sides = ((1, 0), (0, 1))
+    steps = (1, 2, 3)
+    gathered = []
+    for (dx, dy), rows in zip(sides, split(arrived, 2)):
+        gathered.append(jnp.concatenate([rows] + [along_plane(rows, k * dx, k * dy) for k in steps]))
+    after, before = [], []
+    for (dy, dx), rows in zip(sides, gathered):
+        after.append(along_plane(rows, dx, dy))
+        before.append(along_plane(rows, -dx, -dy))
+    after, before = lax.optimization_barrier((after, before))
+    opposite = []
+    for (dy, dx), a, b in zip(sides, after, before):
+        half = a.shape[0] // 2
+        opposite += [along_plane(a[:half], dx, dy), along_plane(b[half:], -dx, -dy)]
+    near_by = split(expert(jnp.concatenate(gathered + after + before), up, down), 6)
+    far_off = split(expert(jnp.concatenate(opposite), up, down), 4)
+    passed = []
+    for i, (dy, dx) in enumerate(sides):
+        passed.append(along_plane(far_off[2 * i], -dx, -dy))
+        passed.append(along_plane(far_off[2 * i + 1], dx, dy))
+    passed = lax.optimization_barrier(passed)
+    sums = []
+    for i, (dy, dx) in enumerate(sides):
+        to_after, to_before = near_by[2 + i], near_by[4 + i]
+        half = to_after.shape[0] // 2
+        one = jnp.concatenate([added(to_after[:half], passed[2 * i]), to_after[half:]])
+        three = jnp.concatenate([to_before[:half], added(to_before[half:], passed[2 * i + 1])])
+        sums.append(added(near_by[i], along_plane(one, -dx, -dy), along_plane(three, dx, dy)))
+    result = []
+    for (dx, dy), total in zip(sides, sums):
+        blocks = split(total, 4)
+        result.append(added(blocks[0], *[along_plane(blocks[k], -k * dx, -k * dy) for k in steps]))
+    return jnp.concatenate(result)
 
 
 def shards(
@@ -261,10 +310,7 @@
         dispatch_table, normed, (((0,), (0,)), ((), ())), preferred_element_type=F32
     ).astype(BF16)
     arrived = lax.all_to_all(outgoing, "exp", split_axis=0, concat_axis=0, tiled=True)
-    segment = lax.all_gather(arrived, "ctx", axis=0, tiled=True)
-    hidden = jax.nn.silu(jnp.dot(segment, up_local, preferred_element_type=F32)).astype(BF16)
-    partial = jnp.dot(hidden, down_local, preferred_element_type=F32).astype(BF16)
-    expert_out = lax.psum_scatter(partial, "ctx", scatter_dimension=0, tiled=True)
+    expert_out = run_expert(arrived, up_local, down_local)
     returned = lax.all_to_all(expert_out, "exp", split_axis=0, concat_axis=0, tiled=True)
     gate_weights = gate_codes.astype(F32)
     gate_weights = gate_weights / jnp.sum(gate_weights, axis=1, keepdims=True)

time: 299 us -> 237 us (0.79); the launches traced: 298 us -> 232 us
  waiting for transfers between devices: 152 us -> 68.5 us
  starting transfers between devices: 30.8 us -> 92.9 us
  blocking collectives: 62.7 us -> 17.3 us
  between operations: 13.6 us -> 0.64 us
  local copies, waits for them, and re-layouts: 6.99 us -> 18.6 us
    reduce_scatter x1 -> x0, waiting for transfers between devices: 80.9 us -> none  [shards(): lax.psum_scatter(partial, 'ctx', scatter_dimension=0, tiled=True)]
    all_gather x1 -> x0, waiting for transfers between devices: 50.6 us -> none  [shards(): segment = lax.all_gather(arrived, 'ctx', axis=0, tiled=True)]
    ppermute x0 -> x34, starting transfers between devices: none -> 49.1 us  [along_plane(): return lax.ppermute(array, 'ctx', pairs)]
    all_gather x2 -> x0, blocking collectives: 45.6 us -> none  [the longest x1 23.2 us: state_space(): parts = lax.all_gather(part, 'exp')]
    ppermute x0 -> x34, waiting for transfers between devices: none -> 37.9 us  [along_plane(): return lax.ppermute(array, 'ctx', pairs)]
    ppermute x8 -> x11, waiting for transfers between devices: 8.59 us -> 18.4 us  [along_depth(): return lax.ppermute(array, 'exp', pairs)]
    unnamed x14 -> x37, local copies, waits for them, and re-layouts: 2.21 us -> 10.8 us
    ppermute x8 -> x11, starting transfers between devices: 17.1 us -> 25.1 us  [along_depth(): return lax.ppermute(array, 'exp', pairs)]
  transfers between devices with their start and end apart: 12 -> 47, of which waited for: 9 -> 28; matrix products, arithmetic and copies ran while one was open for 1% -> 7% of each run, Pallas kernels for 0% -> 0%
where the time goes in v1:
time: 237 us; the launch traced here: 232 us
  starting transfers between devices  92.9 us (39%)
  waiting for transfers between devices  68.5 us (29%)
  local copies, waits for them, and re-layouts  18.6 us (8%)
  matrix products  17.5 us (7%)
  blocking collectives  17.3 us (7%)
  Pallas kernels  12.6 us (5%)
  other arithmetic  4.25 us (2%)
    ppermute x34, starting transfers between devices, along_plane(): return lax.ppermute(array, 'ctx', pairs)  49.1 us
    ppermute x34, waiting for transfers between devices, along_plane(): return lax.ppermute(array, 'ctx', pairs)  37.9 us
    ppermute x11, starting transfers between devices, along_depth(): return lax.ppermute(array, 'exp', pairs)  25.1 us
    ppermute x11, waiting for transfers between devices, along_depth(): return lax.ppermute(array, 'exp', pairs)  18.4 us
    all_to_all x1, blocking collectives, shards(): lax.all_to_all(outgoing, 'exp', split_axis=0, concat_axis=0, tiled=True)  17.3 us
    all_to_all x1, starting transfers between devices, shards(): lax.all_to_all(expert_out, 'exp', split_axis=0, concat_axis=0, tiled=True)  14.7 us
    dot_general x2, matrix products, expert(): return jnp.dot(hidden, down, preferred_element_type=F32).astype(BF16)  14.2 us
    all_to_all x1, waiting for transfers between devices, shards(): lax.all_to_all(expert_out, 'exp', split_axis=0, concat_axis=0, tiled=True)  11.5 us
  transfers between devices with their start and end apart: 47, of which 28 were waited for; matrix products, arithmetic and copies ran while one was open for 7% of the time, Pallas kernels for 0%

profile of v1, /device:TPU:1, one launch (start us, length us, event | category | flops | bytes accessed | tf_op | source)
XLA Modules:
  0.0 232.3 jit_solution(12166881613443885264)
XLA Ops:
  0.7 4.0 %collective-permute-start = (bf16[3,512]{1,0:T(4,128)(2,1)S(1)}, bf16[3,512]{1,0:T(4,128)(2,1)S(1)}, u32[]{:S(2)}, u32[]{:S(2)}) collective-permute-start(bf16[3,512]{1,0:T(4,128)(2,1)S(1)} %slice.129), channel_id=1, source_target_pairs={{0,16},{16,32},{32,48},{48,64},{64,80},{80,96},{96,112},{112,128},... | collective-permute-start | bytes 9224 | tf_op jit(solution)/shard_map/ppermute | solution.py:22
  6.1 1.9 prepare.1
  8.0 1.5 collective-permute-start.1
  9.5 1.7 collective-permute-start.2
  11.2 1.3 collective-permute-done.2
  12.5 2.1 collective-permute-done.3
  15.3 3.1 %collective-permute-start.4 = (f32[32,128]{1,0:T(8,128)S(1)}, f32[32,128]{1,0:T(8,128)S(1)}, u32[]{:S(2)}, u32[]{:S(2)}) collective-permute-start(f32[32,128]{1,0:T(8,128)S(1)} %add_add_fusion.a_ref), channel_id=1, source_target_pairs={{0,4},{1,5},{2,6},{3,7},{4,8},{5,9},{6,10},{7,11},{8,12},{9,13},{1... | collective-permute-start | bytes 49160 | tf_op jit(solution)/shard_map/ppermute | solution.py:40
  18.4 4.2 %collective-permute-start.5 = (f32[32,128]{1,0:T(8,128)S(1)}, f32[32,128]{1,0:T(8,128)S(1)}, u32[]{:S(2)}, u32[]{:S(2)}) collective-permute-start(f32[32,128]{1,0:T(8,128)S(1)} %add_add_fusion.a_ref), channel_id=1, source_target_pairs={{0,8},{1,9},{2,10},{3,11},{4,12},{5,13},{6,14},{7,15},{8,0},{9,1},... | collective-permute-start | bytes 49160 | tf_op jit(solution)/shard_map/ppermute | solution.py:40
  22.5 2.4 %collective-permute-start.6 = (f32[32,128]{1,0:T(8,128)S(1)}, f32[32,128]{1,0:T(8,128)S(1)}, u32[]{:S(2)}, u32[]{:S(2)}) collective-permute-start(f32[32,128]{1,0:T(8,128)S(1)} %add_add_fusion.a_ref), channel_id=1, source_target_pairs={{0,12},{1,13},{2,14},{3,15},{4,0},{5,1},{6,2},{7,3},{8,4},{9,5},{1... | collective-permute-start | bytes 49160 | tf_op jit(solution)/shard_map/ppermute | solution.py:40
  24.9 1.2 collective-permute-done.6.d_ref
  26.7 4.6 %end_state.1 = (f32[32,128]{1,0:T(8,128)}, bf16[32,512]{1,0:T(8,128)(2,1)}) custom-call(f32[32,128]{1,0:T(8,128)} %copy-done.1, f32[32,128]{1,0:T(8,128)} %copy-done.3, f32[32,128]{1,0:T(8,128)} %copy-done.4, f32[32,128]{1,0:T(8,128)} %copy-done.5, s32[128,512]{1,0:T(8,128)} %codes_ref.3, f32[128,512]{1,0:T(8,128)} %get-tuple-element.18.signal_ref, ...), custom_call_target="tpu_custom_call" | custom-call | tf_op jit(solution)/shard_map/end_state/pallas_call | solution.py:181
  31.3 2.0 collective-permute-start.7
  34.1 2.6 %collective-permute-start.8 = (bf16[32,512]{1,0:T(8,128)(2,1)}, bf16[32,512]{1,0:T(8,128)(2,1)S(1)}, u32[]{:S(2)}, u32[]{:S(2)}) collective-permute-start(bf16[32,512]{1,0:T(8,128)(2,1)} %get-tuple-element.19), channel_id=1, source_target_pairs={{0,32},{16,48},{32,0},{48,16},{64,96},{80,112},{96,64},{112,80},{1... | collective-permute-start | bytes 98312 | tf_op jit(solution)/shard_map/ppermute | solution.py:31
  36.7 1.1 collective-permute-start.9
  37.8 0.9 collective-permute-done.8
  38.7 1.1 collective-permute-done.9
  39.8 1.5 collective-permute-start.10
  41.2 2.5 %collective-permute-start.11 = (bf16[128,512]{1,0:T(8,128)(2,1)S(1)}, bf16[128,512]{1,0:T(8,128)(2,1)S(1)}, u32[]{:S(2)}, u32[]{:S(2)}) collective-permute-start(bf16[128,512]{1,0:T(8,128)(2,1)S(1)} %get-tuple-element.74), channel_id=1, source_target_pairs={{0,128},{16,144},{32,160},{48,176},{64,192},{80,208},{96,224},{112... | collective-permute-start | bytes 393224 | tf_op jit(solution)/shard_map/ppermute | solution.py:31
  44.3 1.2 collective-permute-start.12
  45.5 2.0 collective-permute-done.11
  47.5 1.0 collective-permute-done.12
  49.3 6.1 %scan.1 = bf16[128,512]{1,0:T(8,128)(2,1)} custom-call(s32[3]{0:T(128)} %pad_add_fusion.where_ref, bf16[512,512]{1,0:T(8,128)(2,1)} %copy-done, f32[32,128]{1,0:T(8,128)} %get-tuple-element.20.maps_ref, s32[128,512]{1,0:T(8,128)} %codes_ref.3, f32[128,512]{1,0:T(8,128)} %get-tuple-element.18.signal_ref, f32[16,512]{1,0:T(8,128)} %rates_ref.3, ...), custom_call_target="tpu_custom_call" | custom-call | tf_op jit(solution)/shard_map/scan/pallas_call | solution.py:195
  55.4 3.0 %convolution_convert_fusion.2 = bf16[128,4096]{1,0:T(8,128)(2,1)S(1)} fusion(bf16[128,512]{1,0:T(8,128)(2,1)} %scan.1, bf16[512,4096]{1,0:T(8,128)(2,1)} %param.23), kind=kOutput, calls=%fused_computation.3 | convolution fusion | flops 537395200 | bytes 5373952 | tf_op jit(solution)/shard_map/dot_general | solution.py:210
  58.4 4.8 %collective-permute-start.13 = (bf16[64,4096]{1,0:T(8,128)(2,1)S(1)}, bf16[64,4096]{1,0:T(8,128)(2,1)S(1)}, u32[]{:S(2)}, u32[]{:S(2)}) collective-permute-start(bf16[64,4096]{1,0:T(8,128)(2,1)S(1)} %slice.171), channel_id=1, source_target_pairs={{0,1},{1,0},{2,3},{3,2},{4,5},{5,4},{6,7},{7,6},{8,9},{9,8},{10,11... | collective-permute-start | bytes 1572872 | tf_op jit(solution)/shard_map/ppermute | solution.py:40
  63.5 1.3 collective-permute-done.13
  66.1 6.4 %collective-permute-done.14 = bf16[32,4096]{1,0:T(8,128)(2,1)S(1)} collective-permute-done((bf16[32,4096]{1,0:T(8,128)(2,1)S(1)}, bf16[32,4096]{1,0:T(8,128)(2,1)S(1)}, u32[]{:S(2)}, u32[]{:S(2)}) %collective-permute-start.14) | collective-permute-done | bytes 262176 | tf_op jit(solution)/shard_map/ppermute | solution.py:40
  72.6 1.9 collective-permute-start.15
  74.6 4.2 %collective-permute-start.16 = (bf16[8,4096]{1,0:T(8,128)(2,1)S(1)}, bf16[8,4096]{1,0:T(8,128)(2,1)S(1)}, u32[]{:S(2)}, u32[]{:S(2)}) collective-permute-start(bf16[8,4096]{1,0:T(8,128)(2,1)S(1)} %get-tuple-element.57), channel_id=1, source_target_pairs={{0,8},{1,9},{2,10},{3,11},{4,12},{5,13},{6,14},{7,15},{8,0},{9,1},... | collective-permute-start | bytes 196616 | tf_op jit(solution)/shard_map/ppermute | solution.py:40
  79.4 4.4 %collective-permute-done.16 = bf16[8,4096]{1,0:T(8,128)(2,1)S(1)} collective-permute-done((bf16[8,4096]{1,0:T(8,128)(2,1)S(1)}, bf16[8,4096]{1,0:T(8,128)(2,1)S(1)}, u32[]{:S(2)}, u32[]{:S(2)}) %collective-permute-start.16) | collective-permute-done | bytes 65568 | tf_op jit(solution)/shard_map/ppermute | solution.py:40
  83.7 1.8 collective-permute-done.17
  86.1 17.3 %all_to_all.21 = bf16[16,2,4096]{2,1,0:T(2,128)(2,1)S(1)} all-to-all(bf16[16,2,4096]{2,1,0:T(2,128)(2,1)S(1)} %all_to_all.14), channel_id=1, replica_groups=mesh['ctx'=16,'exp'=16] {'exp'}, dimensions={0} | all-to-all | bytes 524288 | tf_op jit(solution)/shard_map/all_to_all | solution.py:312
  103.7 1.0 collective-permute-start.18
  105.4 3.0 %collective-permute-start.19 = (bf16[16,4096]{1,0:T(8,128)(2,1)S(1)}, bf16[16,4096]{1,0:T(8,128)(2,1)S(1)}, u32[]{:S(2)}, u32[]{:S(2)}) collective-permute-start(bf16[16,4096]{1,0:T(8,128)(2,1)S(1)} %slice.139), channel_id=1, source_target_pairs={{0,128},{16,144},{32,160},{48,176},{64,192},{80,208},{96,224},{112... | collective-permute-start | bytes 393224 | tf_op jit(solution)/shard_map/ppermute | solution.py:31
  108.5 1.5 collective-permute-start.21
  110.0 2.2 collective-permute-start.22
  113.7 0.9 collective-permute-done.19
  117.3 1.2 collective-permute-done.22
  119.8 1.2 collective-permute-start.25
  121.0 1.5 collective-permute-start.27
  123.2 2.0 collective-permute-start.26
  125.2 8.3 %collective-permute-done.25 = bf16[64,4096]{1,0:T(8,128)(2,1)S(1)} collective-permute-done((bf16[64,4096]{1,0:T(8,128)(2,1)S(1)}, bf16[64,4096]{1,0:T(8,128)(2,1)S(1)}, u32[]{:S(2)}, u32[]{:S(2)}) %collective-permute-start.25) | collective-permute-done | bytes 524320 | tf_op jit(solution)/shard_map/ppermute | solution.py:31
  133.4 2.1 collective-permute-done.24
  141.3 2.5 %collective-permute-start.29 = (bf16[32,4096]{1,0:T(8,128)(2,1)}, bf16[32,4096]{1,0:T(8,128)(2,1)}, u32[]{:S(2)}, u32[]{:S(2)}) collective-permute-start(bf16[32,4096]{1,0:T(8,128)(2,1)} %slice.145), channel_id=1, source_target_pairs={{0,48},{16,0},{32,16},{48,32},{64,112},{80,64},{96,80},{112,96},{1... | collective-permute-start | bytes 786440 | tf_op jit(solution)/shard_map/ppermute | solution.py:31
  143.8 11.3 %collective-permute-start.31 = (bf16[32,4096]{1,0:T(8,128)(2,1)}, bf16[32,4096]{1,0:T(8,128)(2,1)}, u32[]{:S(2)}, u32[]{:S(2)}) collective-permute-start(bf16[32,4096]{1,0:T(8,128)(2,1)} %slice.147), channel_id=1, source_target_pairs={{0,192},{16,208},{32,224},{48,240},{64,0},{80,16},{96,32},{112,48}... | collective-permute-start | bytes 786440 | tf_op jit(solution)/shard_map/ppermute | solution.py:31
  155.1 7.9 %convolution_convert_fusion = bf16[384,4096]{1,0:T(8,128)(2,1)S(1)} fusion(bf16[1,512,4096]{2,1,0:T(8,128)(2,1)} %param.29, bf16[384,4096]{1,0:T(8,128)(2,1)} %constant_dynamic-update-slice_fusion.19, bf16[1,4096,512]{2,1,0:T(8,128)(2,1)} %param.28), kind=kOutput, calls=%fused_computation.1 | convolution fusion | flops 3223781376 | bytes 14680064 | tf_op jit(solution)/shard_map/dot_general | solution.py:221
  163.0 6.3 %convolution_convert_fusion.1 = bf16[128,4096]{1,0:T(8,128)(2,1)} fusion(bf16[1,512,4096]{2,1,0:T(8,128)(2,1)} %param.29, bf16[1,4096,512]{2,1,0:T(8,128)(2,1)} %param.28, bf16[32,4096]{1,0:T(8,128)(2,1)} %collective-permute-done.31, bf16[32,4096]{1,0:T(8,128)(2,1)} %collective-permute-done.30, bf16[32,4096]{1,0:T(8,128)(2,1)} %collective-permute-done.29, ...), kind=kOutput, calls=%fused_computation.2 | convolution fusion | flops 1078788096 | bytes 10485760 | tf_op jit(solution)/shard_map/dot_general | solution.py:221
  169.3 1.3 fusion.41
  170.6 1.3 collective-permute-start.32
  172.1 1.5 collective-permute-start.35
  173.7 2.2 collective-permute-done.32
  175.9 2.4 %collective-permute-done.33 = bf16[32,4096]{1,0:T(8,128)(2,1)S(1)} collective-permute-done((bf16[32,4096]{1,0:T(8,128)(2,1)S(1)}, bf16[32,4096]{1,0:T(8,128)(2,1)S(1)}, u32[]{:S(2)}, u32[]{:S(2)}) %collective-permute-start.33) | collective-permute-done | bytes 262176 | tf_op jit(solution)/shard_map/ppermute | solution.py:31
  179.0 1.5 collective-permute-start.42
  180.6 2.8 %collective-permute-start.36 = (bf16[64,4096]{1,0:T(8,128)(2,1)S(1)}, bf16[64,4096]{1,0:T(8,128)(2,1)S(1)}, u32[]{:S(2)}, u32[]{:S(2)}) collective-permute-start(bf16[64,4096]{1,0:T(8,128)(2,1)S(1)} %pad_maximum_fusion), channel_id=1, source_target_pairs={{0,48},{16,0},{32,16},{48,32},{64,112},{80,64},{96,80},{112,96},{1... | collective-permute-start | bytes 1572872 | tf_op jit(solution)/shard_map/ppermute | solution.py:31
  183.5 4.1 %collective-permute-done.41 = bf16[64,4096]{1,0:T(8,128)(2,1)S(1)} collective-permute-done((bf16[64,4096]{1,0:T(8,128)(2,1)S(1)}, bf16[64,4096]{1,0:T(8,128)(2,1)S(1)}, u32[]{:S(2)}, u32[]{:S(2)}) %collective-permute-start.41) | collective-permute-done | bytes 524320 | tf_op jit(solution)/shard_map/ppermute | solution.py:31
  187.6 1.2 collective-permute-done.42
  189.5 3.5 %collective-permute-done.37 = bf16[64,4096]{1,0:T(8,128)(2,1)S(1)} collective-permute-done((bf16[64,4096]{1,0:T(8,128)(2,1)S(1)}, bf16[64,4096]{1,0:T(8,128)(2,1)S(1)}, u32[]{:S(2)}, u32[]{:S(2)}) %collective-permute-start.37) | collective-permute-done | bytes 524320 | tf_op jit(solution)/shard_map/ppermute | solution.py:31
  193.5 1.3 collective-permute-start.38
  196.5 1.2 collective-permute-done.38
  197.7 2.7 %collective-permute-done.39 = bf16[16,4096]{1,0:T(8,128)(2,1)S(1)} collective-permute-done((bf16[16,4096]{1,0:T(8,128)(2,1)S(1)}, bf16[16,4096]{1,0:T(8,128)(2,1)S(1)}, u32[]{:S(2)}, u32[]{:S(2)}) %collective-permute-start.39) | collective-permute-done | bytes 131104 | tf_op jit(solution)/shard_map/ppermute | solution.py:31
  200.5 1.3 collective-permute-done.40
  201.9 0.9 collective-permute-done.45
  202.8 0.9 all_to_all.16
  203.7 14.7 %all-to-all-start.1 = ((bf16[16,2,4096]{2,1,0:T(2,128)(2,1)}), bf16[16,2,4096]{2,1,0:T(2,128)(2,1)S(1)}, u32[]{:S(2)}, u32[]{:S(2)}) async-start(bf16[16,2,4096]{2,1,0:T(2,128)(2,1)} %all_to_all.16), calls=%async_computation.1 | async-start | bytes 524288 | tf_op jit(solution)/shard_map/all_to_all | solution.py:314
  218.6 11.5 %all-to-all-done.1 = bf16[16,2,4096]{2,1,0:T(2,128)(2,1)S(1)} async-done(((bf16[16,2,4096]{2,1,0:T(2,128)(2,1)}), bf16[16,2,4096]{2,1,0:T(2,128)(2,1)S(1)}, u32[]{:S(2)}, u32[]{:S(2)}) %all-to-all-start.1) | async-done | bytes 262176 | tf_op jit(solution)/shard_map/all_to_all | solution.py:314
  (129 shorter events, 27.9 us)
Async XLA Ops:
  0.7 4.8 %collective-permute-start = (bf16[3,512]{1,0:T(4,128)(2,1)S(1)}, bf16[3,512]{1,0:T(4,128)(2,1)S(1)}, u32[]{:S(2)}, u32[]{:S(2)}) collective-permute-start(bf16[3,512]{1,0:T(4,128)(2,1)S(1)} %slice.129), channel_id=1, source_target_pairs={{0,16},{16,32},{32,48},{48,64},{64,80},{80,96},{96,112},{112,128},... | collective-permute-start | bytes 9224 | tf_op jit(solution)/shard_map/ppermute | solution.py:22
  5.5 0.6 copy-start.7
  8.0 3.2 %collective-permute-start.1 = (f32[32,128]{1,0:T(8,128)}, f32[32,128]{1,0:T(8,128)S(1)}, u32[]{:S(2)}, u32[]{:S(2)}) collective-permute-start(f32[32,128]{1,0:T(8,128)} %get-tuple-element.17), channel_id=1, source_target_pairs={{0,1},{1,0},{2,3},{3,2},{4,5},{5,4},{6,7},{7,6},{8,9},{9,8},{10,11... | collective-permute-start | bytes 49160 | tf_op jit(solution)/shard_map/ppermute | solution.py:40
  9.5 3.0 %collective-permute-start.2 = (f32[32,128]{1,0:T(8,128)}, f32[32,128]{1,0:T(8,128)S(1)}, u32[]{:S(2)}, u32[]{:S(2)}) collective-permute-start(f32[32,128]{1,0:T(8,128)} %get-tuple-element.17), channel_id=1, source_target_pairs={{0,2},{1,3},{2,0},{3,1},{4,6},{5,7},{6,4},{7,5},{8,10},{9,11},{10,... | collective-permute-start | bytes 49160 | tf_op jit(solution)/shard_map/ppermute | solution.py:40
  11.2 3.4 %collective-permute-start.3 = (f32[32,128]{1,0:T(8,128)}, f32[32,128]{1,0:T(8,128)S(1)}, u32[]{:S(2)}, u32[]{:S(2)}) collective-permute-start(f32[32,128]{1,0:T(8,128)} %get-tuple-element.17), channel_id=1, source_target_pairs={{0,3},{1,2},{2,1},{3,0},{4,7},{5,6},{6,5},{7,4},{8,11},{9,10},{10,... | collective-permute-start | bytes 49160 | tf_op jit(solution)/shard_map/ppermute | solution.py:40
  15.3 10.9 %copy-start.1 = (f32[32,128]{1,0:T(8,128)}, f32[32,128]{1,0:T(8,128)S(1)}, u32[]{:S(2)}) copy-start(f32[32,128]{1,0:T(8,128)S(1)} %add_add_fusion.a_ref) | copy-start | bytes 49156
  15.3 9.6 %collective-permute-start.4 = (f32[32,128]{1,0:T(8,128)S(1)}, f32[32,128]{1,0:T(8,128)S(1)}, u32[]{:S(2)}, u32[]{:S(2)}) collective-permute-start(f32[32,128]{1,0:T(8,128)S(1)} %add_add_fusion.a_ref), channel_id=1, source_target_pairs={{0,4},{1,5},{2,6},{3,7},{4,8},{5,9},{6,10},{7,11},{8,12},{9,13},{1... | collective-permute-start | bytes 49160 | tf_op jit(solution)/shard_map/ppermute | solution.py:40
  18.4 6.6 %collective-permute-start.5 = (f32[32,128]{1,0:T(8,128)S(1)}, f32[32,128]{1,0:T(8,128)S(1)}, u32[]{:S(2)}, u32[]{:S(2)}) collective-permute-start(f32[32,128]{1,0:T(8,128)S(1)} %add_add_fusion.a_ref), channel_id=1, source_target_pairs={{0,8},{1,9},{2,10},{3,11},{4,12},{5,13},{6,14},{7,15},{8,0},{9,1},... | collective-permute-start | bytes 49160 | tf_op jit(solution)/shard_map/ppermute | solution.py:40
  22.5 3.6 %collective-permute-start.6 = (f32[32,128]{1,0:T(8,128)S(1)}, f32[32,128]{1,0:T(8,128)S(1)}, u32[]{:S(2)}, u32[]{:S(2)}) collective-permute-start(f32[32,128]{1,0:T(8,128)S(1)} %add_add_fusion.a_ref), channel_id=1, source_target_pairs={{0,12},{1,13},{2,14},{3,15},{4,0},{5,1},{6,2},{7,3},{8,4},{9,5},{1... | collective-permute-start | bytes 49160 | tf_op jit(solution)/shard_map/ppermute | solution.py:40
  24.9 1.2 copy-start.3
  24.9 1.2 copy-start.4
  26.1 0.6 copy-start.5
  31.3 6.5 %collective-permute-start.7 = (bf16[32,512]{1,0:T(8,128)(2,1)}, bf16[32,512]{1,0:T(8,128)(2,1)S(1)}, u32[]{:S(2)}, u32[]{:S(2)}) collective-permute-start(bf16[32,512]{1,0:T(8,128)(2,1)} %get-tuple-element.19), channel_id=1, source_target_pairs={{0,16},{16,32},{32,48},{48,0},{64,80},{80,96},{96,112},{112,64},{1... | collective-permute-start | bytes 98312 | tf_op jit(solution)/shard_map/ppermute | solution.py:31
  34.1 4.6 %collective-permute-start.8 = (bf16[32,512]{1,0:T(8,128)(2,1)}, bf16[32,512]{1,0:T(8,128)(2,1)S(1)}, u32[]{:S(2)}, u32[]{:S(2)}) collective-permute-start(bf16[32,512]{1,0:T(8,128)(2,1)} %get-tuple-element.19), channel_id=1, source_target_pairs={{0,32},{16,48},{32,0},{48,16},{64,96},{80,112},{96,64},{112,80},{1... | collective-permute-start | bytes 98312 | tf_op jit(solution)/shard_map/ppermute | solution.py:31
  36.7 3.1 %collective-permute-start.9 = (bf16[32,512]{1,0:T(8,128)(2,1)}, bf16[32,512]{1,0:T(8,128)(2,1)S(1)}, u32[]{:S(2)}, u32[]{:S(2)}) collective-permute-start(bf16[32,512]{1,0:T(8,128)(2,1)} %get-tuple-element.19), channel_id=1, source_target_pairs={{0,48},{16,0},{32,16},{48,32},{64,112},{80,64},{96,80},{112,96},{1... | collective-permute-start | bytes 98312 | tf_op jit(solution)/shard_map/ppermute | solution.py:31
  39.8 5.7 %collective-permute-start.10 = (bf16[128,512]{1,0:T(8,128)(2,1)S(1)}, bf16[128,512]{1,0:T(8,128)(2,1)S(1)}, u32[]{:S(2)}, u32[]{:S(2)}) collective-permute-start(bf16[128,512]{1,0:T(8,128)(2,1)S(1)} %get-tuple-element.74), channel_id=1, source_target_pairs={{0,64},{16,80},{32,96},{48,112},{64,128},{80,144},{96,160},{112,17... | collective-permute-start | bytes 393224 | tf_op jit(solution)/shard_map/ppermute | solution.py:31
  41.2 6.2 %collective-permute-start.11 = (bf16[128,512]{1,0:T(8,128)(2,1)S(1)}, bf16[128,512]{1,0:T(8,128)(2,1)S(1)}, u32[]{:S(2)}, u32[]{:S(2)}) collective-permute-start(bf16[128,512]{1,0:T(8,128)(2,1)S(1)} %get-tuple-element.74), channel_id=1, source_target_pairs={{0,128},{16,144},{32,160},{48,176},{64,192},{80,208},{96,224},{112... | collective-permute-start | bytes 393224 | tf_op jit(solution)/shard_map/ppermute | solution.py:31
  44.3 4.1 %collective-permute-start.12 = (bf16[128,512]{1,0:T(8,128)(2,1)S(1)}, bf16[128,512]{1,0:T(8,128)(2,1)S(1)}, u32[]{:S(2)}, u32[]{:S(2)}) collective-permute-start(bf16[128,512]{1,0:T(8,128)(2,1)S(1)} %get-tuple-element.74), channel_id=1, source_target_pairs={{0,192},{16,208},{32,224},{48,240},{64,0},{80,16},{96,32},{112,48}... | collective-permute-start | bytes 393224 | tf_op jit(solution)/shard_map/ppermute | solution.py:31
  48.4 0.8 copy-start
  55.4 7.9 %copy-start.8 = (s32[8,2]{0,1:T(2,128)S(1)}, s32[8,2]{0,1:T(2,128)}, u32[]{:S(2)}) copy-start(s32[8,2]{0,1:T(2,128)} %param.26) | copy-start | bytes 196
  58.4 27.1 %copy-start.2 = (bf16[8,4096]{1,0:T(8,128)(2,1)S(1)}, bf16[8,4096]{1,0:T(8,128)(2,1)}, u32[]{:S(2)}) copy-start(bf16[8,4096]{1,0:T(8,128)(2,1)} %param.24) | copy-start | bytes 196612
  58.4 27.3 %copy-start.6 = (f32[4096]{0:T(1024)S(1)}, f32[4096]{0:T(1024)}, u32[]{:S(2)}) copy-start(f32[4096]{0:T(1024)} %param.25) | copy-start | bytes 49156
  58.4 6.3 %collective-permute-start.13 = (bf16[64,4096]{1,0:T(8,128)(2,1)S(1)}, bf16[64,4096]{1,0:T(8,128)(2,1)S(1)}, u32[]{:S(2)}, u32[]{:S(2)}) collective-permute-start(bf16[64,4096]{1,0:T(8,128)(2,1)S(1)} %slice.171), channel_id=1, source_target_pairs={{0,1},{1,0},{2,3},{3,2},{4,5},{5,4},{6,7},{7,6},{8,9},{9,8},{10,11... | collective-permute-start | bytes 1572872 | tf_op jit(solution)/shard_map/ppermute | solution.py:40
  64.9 7.6 %collective-permute-start.14 = (bf16[32,4096]{1,0:T(8,128)(2,1)S(1)}, bf16[32,4096]{1,0:T(8,128)(2,1)S(1)}, u32[]{:S(2)}, u32[]{:S(2)}) collective-permute-start(bf16[32,4096]{1,0:T(8,128)(2,1)S(1)} %slice.173), channel_id=1, source_target_pairs={{0,2},{1,3},{2,0},{3,1},{4,6},{5,7},{6,4},{7,5},{8,10},{9,11},{10,... | collective-permute-start | bytes 786440 | tf_op jit(solution)/shard_map/ppermute | solution.py:40
  72.6 6.7 %collective-permute-start.15 = (bf16[8,4096]{1,0:T(8,128)(2,1)S(1)}, bf16[8,4096]{1,0:T(8,128)(2,1)S(1)}, u32[]{:S(2)}, u32[]{:S(2)}) collective-permute-start(bf16[8,4096]{1,0:T(8,128)(2,1)S(1)} %get-tuple-element.55), channel_id=1, source_target_pairs={{0,4},{1,5},{2,6},{3,7},{4,8},{5,9},{6,10},{7,11},{8,12},{9,13},{1... | collective-permute-start | bytes 196616 | tf_op jit(solution)/shard_map/ppermute | solution.py:40
  74.6 9.2 %collective-permute-start.16 = (bf16[8,4096]{1,0:T(8,128)(2,1)S(1)}, bf16[8,4096]{1,0:T(8,128)(2,1)S(1)}, u32[]{:S(2)}, u32[]{:S(2)}) collective-permute-start(bf16[8,4096]{1,0:T(8,128)(2,1)S(1)} %get-tuple-element.57), channel_id=1, source_target_pairs={{0,8},{1,9},{2,10},{3,11},{4,12},{5,13},{6,14},{7,15},{8,0},{9,1},... | collective-permute-start | bytes 196616 | tf_op jit(solution)/shard_map/ppermute | solution.py:40
  78.7 6.8 %collective-permute-start.17 = (bf16[8,4096]{1,0:T(8,128)(2,1)S(1)}, bf16[8,4096]{1,0:T(8,128)(2,1)S(1)}, u32[]{:S(2)}, u32[]{:S(2)}) collective-permute-start(bf16[8,4096]{1,0:T(8,128)(2,1)S(1)} %get-tuple-element.56), channel_id=1, source_target_pairs={{0,12},{1,13},{2,14},{3,15},{4,0},{5,1},{6,2},{7,3},{8,4},{9,5},{1... | collective-permute-start | bytes 196616 | tf_op jit(solution)/shard_map/ppermute | solution.py:40
  103.7 8.5 %collective-permute-start.18 = (bf16[16,4096]{1,0:T(8,128)(2,1)S(1)}, bf16[16,4096]{1,0:T(8,128)(2,1)S(1)}, u32[]{:S(2)}, u32[]{:S(2)}) collective-permute-start(bf16[16,4096]{1,0:T(8,128)(2,1)S(1)} %slice.139), channel_id=1, source_target_pairs={{0,64},{16,80},{32,96},{48,112},{64,128},{80,144},{96,160},{112,17... | collective-permute-start | bytes 393224 | tf_op jit(solution)/shard_map/ppermute | solution.py:31
  105.4 9.2 %collective-permute-start.19 = (bf16[16,4096]{1,0:T(8,128)(2,1)S(1)}, bf16[16,4096]{1,0:T(8,128)(2,1)S(1)}, u32[]{:S(2)}, u32[]{:S(2)}) collective-permute-start(bf16[16,4096]{1,0:T(8,128)(2,1)S(1)} %slice.139), channel_id=1, source_target_pairs={{0,128},{16,144},{32,160},{48,176},{64,192},{80,208},{96,224},{112... | collective-permute-start | bytes 393224 | tf_op jit(solution)/shard_map/ppermute | solution.py:31
  108.4 6.8 %collective-permute-start.20 = (bf16[16,4096]{1,0:T(8,128)(2,1)S(1)}, bf16[16,4096]{1,0:T(8,128)(2,1)S(1)}, u32[]{:S(2)}, u32[]{:S(2)}) collective-permute-start(bf16[16,4096]{1,0:T(8,128)(2,1)S(1)} %slice.139), channel_id=1, source_target_pairs={{0,192},{16,208},{32,224},{48,240},{64,0},{80,16},{96,32},{112,48}... | collective-permute-start | bytes 393224 | tf_op jit(solution)/shard_map/ppermute | solution.py:31
  108.5 8.1 %collective-permute-start.21 = (bf16[16,4096]{1,0:T(8,128)(2,1)S(1)}, bf16[16,4096]{1,0:T(8,128)(2,1)S(1)}, u32[]{:S(2)}, u32[]{:S(2)}) collective-permute-start(bf16[16,4096]{1,0:T(8,128)(2,1)S(1)} %slice.141), channel_id=1, source_target_pairs={{0,16},{16,32},{32,48},{48,0},{64,80},{80,96},{96,112},{112,64},{1... | collective-permute-start | bytes 393224 | tf_op jit(solution)/shard_map/ppermute | solution.py:31
  110.0 8.5 %collective-permute-start.22 = (bf16[16,4096]{1,0:T(8,128)(2,1)S(1)}, bf16[16,4096]{1,0:T(8,128)(2,1)S(1)}, u32[]{:S(2)}, u32[]{:S(2)}) collective-permute-start(bf16[16,4096]{1,0:T(8,128)(2,1)S(1)} %slice.141), channel_id=1, source_target_pairs={{0,32},{16,48},{32,0},{48,16},{64,96},{80,112},{96,64},{112,80},{1... | collective-permute-start | bytes 393224 | tf_op jit(solution)/shard_map/ppermute | solution.py:31
  112.2 6.9 %collective-permute-start.23 = (bf16[16,4096]{1,0:T(8,128)(2,1)S(1)}, bf16[16,4096]{1,0:T(8,128)(2,1)S(1)}, u32[]{:S(2)}, u32[]{:S(2)}) collective-permute-start(bf16[16,4096]{1,0:T(8,128)(2,1)S(1)} %slice.141), channel_id=1, source_target_pairs={{0,48},{16,0},{32,16},{48,32},{64,112},{80,64},{96,80},{112,96},{1... | collective-permute-start | bytes 393224 | tf_op jit(solution)/shard_map/ppermute | solution.py:31
  119.8 13.6 %collective-permute-start.25 = (bf16[64,4096]{1,0:T(8,128)(2,1)S(1)}, bf16[64,4096]{1,0:T(8,128)(2,1)S(1)}, u32[]{:S(2)}, u32[]{:S(2)}) collective-permute-start(bf16[64,4096]{1,0:T(8,128)(2,1)S(1)} %get-tuple-element.59), channel_id=1, source_target_pairs={{0,64},{16,80},{32,96},{48,112},{64,128},{80,144},{96,160},{112,17... | collective-permute-start | bytes 1572872 | tf_op jit(solution)/shard_map/ppermute | solution.py:31
  121.0 12.4 %collective-permute-start.27 = (bf16[64,4096]{1,0:T(8,128)(2,1)S(1)}, bf16[64,4096]{1,0:T(8,128)(2,1)S(1)}, u32[]{:S(2)}, u32[]{:S(2)}) collective-permute-start(bf16[64,4096]{1,0:T(8,128)(2,1)S(1)} %get-tuple-element.59), channel_id=1, source_target_pairs={{0,192},{16,208},{32,224},{48,240},{64,0},{80,16},{96,32},{112,48}... | collective-permute-start | bytes 1572872 | tf_op jit(solution)/shard_map/ppermute | solution.py:31
  122.5 13.1 %collective-permute-start.24 = (bf16[64,4096]{1,0:T(8,128)(2,1)S(1)}, bf16[64,4096]{1,0:T(8,128)(2,1)S(1)}, u32[]{:S(2)}, u32[]{:S(2)}) collective-permute-start(bf16[64,4096]{1,0:T(8,128)(2,1)S(1)} %get-tuple-element.67), channel_id=1, source_target_pairs={{0,16},{16,32},{32,48},{48,0},{64,80},{80,96},{96,112},{112,64},{1... | collective-permute-start | bytes 1572872 | tf_op jit(solution)/shard_map/ppermute | solution.py:31
  123.2 12.4 %collective-permute-start.26 = (bf16[64,4096]{1,0:T(8,128)(2,1)S(1)}, bf16[64,4096]{1,0:T(8,128)(2,1)S(1)}, u32[]{:S(2)}, u32[]{:S(2)}) collective-permute-start(bf16[64,4096]{1,0:T(8,128)(2,1)S(1)} %get-tuple-element.67), channel_id=1, source_target_pairs={{0,48},{16,0},{32,16},{48,32},{64,112},{80,64},{96,80},{112,96},{1... | collective-permute-start | bytes 1572872 | tf_op jit(solution)/shard_map/ppermute | solution.py:31
  141.1 21.9 %collective-permute-start.28 = (bf16[32,4096]{1,0:T(8,128)(2,1)}, bf16[32,4096]{1,0:T(8,128)(2,1)}, u32[]{:S(2)}, u32[]{:S(2)}) collective-permute-start(bf16[32,4096]{1,0:T(8,128)(2,1)} %slice.144), channel_id=1, source_target_pairs={{0,16},{16,32},{32,48},{48,0},{64,80},{80,96},{96,112},{112,64},{1... | collective-permute-start | bytes 786440 | tf_op jit(solution)/shard_map/ppermute | solution.py:31
  141.3 21.7 %collective-permute-start.29 = (bf16[32,4096]{1,0:T(8,128)(2,1)}, bf16[32,4096]{1,0:T(8,128)(2,1)}, u32[]{:S(2)}, u32[]{:S(2)}) collective-permute-start(bf16[32,4096]{1,0:T(8,128)(2,1)} %slice.145), channel_id=1, source_target_pairs={{0,48},{16,0},{32,16},{48,32},{64,112},{80,64},{96,80},{112,96},{1... | collective-permute-start | bytes 786440 | tf_op jit(solution)/shard_map/ppermute | solution.py:31
  143.8 19.3 %collective-permute-start.30 = (bf16[32,4096]{1,0:T(8,128)(2,1)S(1)}, bf16[32,4096]{1,0:T(8,128)(2,1)}, u32[]{:S(2)}, u32[]{:S(2)}) collective-permute-start(bf16[32,4096]{1,0:T(8,128)(2,1)S(1)} %slice.146), channel_id=1, source_target_pairs={{0,64},{16,80},{32,96},{48,112},{64,128},{80,144},{96,160},{112,17... | collective-permute-start | bytes 786440 | tf_op jit(solution)/shard_map/ppermute | solution.py:31
  143.8 19.3 %collective-permute-start.31 = (bf16[32,4096]{1,0:T(8,128)(2,1)}, bf16[32,4096]{1,0:T(8,128)(2,1)}, u32[]{:S(2)}, u32[]{:S(2)}) collective-permute-start(bf16[32,4096]{1,0:T(8,128)(2,1)} %slice.147), channel_id=1, source_target_pairs={{0,192},{16,208},{32,224},{48,240},{64,0},{80,16},{96,32},{112,48}... | collective-permute-start | bytes 786440 | tf_op jit(solution)/shard_map/ppermute | solution.py:31
  170.6 5.3 %collective-permute-start.32 = (bf16[32,4096]{1,0:T(8,128)(2,1)S(1)}, bf16[32,4096]{1,0:T(8,128)(2,1)S(1)}, u32[]{:S(2)}, u32[]{:S(2)}) collective-permute-start(bf16[32,4096]{1,0:T(8,128)(2,1)S(1)} %get-tuple-element.46), channel_id=1, source_target_pairs={{0,48},{16,0},{32,16},{48,32},{64,112},{80,64},{96,80},{112,96},{1... | collective-permute-start | bytes 786440 | tf_op jit(solution)/shard_map/ppermute | solution.py:31
  171.8 6.4 %collective-permute-start.33 = (bf16[32,4096]{1,0:T(8,128)(2,1)S(1)}, bf16[32,4096]{1,0:T(8,128)(2,1)S(1)}, u32[]{:S(2)}, u32[]{:S(2)}) collective-permute-start(bf16[32,4096]{1,0:T(8,128)(2,1)S(1)} %get-tuple-element.45), channel_id=1, source_target_pairs={{0,16},{16,32},{32,48},{48,0},{64,80},{80,96},{96,112},{112,64},{1... | collective-permute-start | bytes 786440 | tf_op jit(solution)/shard_map/ppermute | solution.py:31
  172.1 6.1 %collective-permute-start.34 = (bf16[32,4096]{1,0:T(8,128)(2,1)S(1)}, bf16[32,4096]{1,0:T(8,128)(2,1)S(1)}, u32[]{:S(2)}, u32[]{:S(2)}) collective-permute-start(bf16[32,4096]{1,0:T(8,128)(2,1)S(1)} %get-tuple-element.44), channel_id=1, source_target_pairs={{0,192},{16,208},{32,224},{48,240},{64,0},{80,16},{96,32},{112,48}... | collective-permute-start | bytes 786440 | tf_op jit(solution)/shard_map/ppermute | solution.py:31
  172.1 6.4 %collective-permute-start.35 = (bf16[32,4096]{1,0:T(8,128)(2,1)S(1)}, bf16[32,4096]{1,0:T(8,128)(2,1)S(1)}, u32[]{:S(2)}, u32[]{:S(2)}) collective-permute-start(bf16[32,4096]{1,0:T(8,128)(2,1)S(1)} %get-tuple-element.43), channel_id=1, source_target_pairs={{0,64},{16,80},{32,96},{48,112},{64,128},{80,144},{96,160},{112,17... | collective-permute-start | bytes 786440 | tf_op jit(solution)/shard_map/ppermute | solution.py:31
  178.9 8.7 %collective-permute-start.41 = (bf16[64,4096]{1,0:T(8,128)(2,1)S(1)}, bf16[64,4096]{1,0:T(8,128)(2,1)S(1)}, u32[]{:S(2)}, u32[]{:S(2)}) collective-permute-start(bf16[64,4096]{1,0:T(8,128)(2,1)S(1)} %pad_maximum_fusion.2), channel_id=1, source_target_pairs={{0,192},{16,208},{32,224},{48,240},{64,0},{80,16},{96,32},{112,48}... | collective-permute-start | bytes 1572872 | tf_op jit(solution)/shard_map/ppermute | solution.py:31
  179.0 9.8 %collective-permute-start.42 = (bf16[64,4096]{1,0:T(8,128)(2,1)S(1)}, bf16[64,4096]{1,0:T(8,128)(2,1)S(1)}, u32[]{:S(2)}, u32[]{:S(2)}) collective-permute-start(bf16[64,4096]{1,0:T(8,128)(2,1)S(1)} %pad_maximum_fusion.3), channel_id=1, source_target_pairs={{0,64},{16,80},{32,96},{48,112},{64,128},{80,144},{96,160},{112,17... | collective-permute-start | bytes 1572872 | tf_op jit(solution)/shard_map/ppermute | solution.py:31
  180.6 8.9 %collective-permute-start.36 = (bf16[64,4096]{1,0:T(8,128)(2,1)S(1)}, bf16[64,4096]{1,0:T(8,128)(2,1)S(1)}, u32[]{:S(2)}, u32[]{:S(2)}) collective-permute-start(bf16[64,4096]{1,0:T(8,128)(2,1)S(1)} %pad_maximum_fusion), channel_id=1, source_target_pairs={{0,48},{16,0},{32,16},{48,32},{64,112},{80,64},{96,80},{112,96},{1... | collective-permute-start | bytes 1572872 | tf_op jit(solution)/shard_map/ppermute | solution.py:31
  183.4 9.6 %collective-permute-start.37 = (bf16[64,4096]{1,0:T(8,128)(2,1)S(1)}, bf16[64,4096]{1,0:T(8,128)(2,1)S(1)}, u32[]{:S(2)}, u32[]{:S(2)}) collective-permute-start(bf16[64,4096]{1,0:T(8,128)(2,1)S(1)} %pad_maximum_fusion.1), channel_id=1, source_target_pairs={{0,16},{16,32},{32,48},{48,0},{64,80},{80,96},{96,112},{112,64},{1... | collective-permute-start | bytes 1572872 | tf_op jit(solution)/shard_map/ppermute | solution.py:31
  193.5 25.0 %copy-start.9 = (s32[8,2]{0,1:T(2,128)S(1)}, s32[8,2]{0,1:T(2,128)}, u32[]{:S(2)}) copy-start(s32[8,2]{0,1:T(2,128)} %param.27) | copy-start | bytes 196
  193.5 4.2 %collective-permute-start.38 = (bf16[16,4096]{1,0:T(8,128)(2,1)S(1)}, bf16[16,4096]{1,0:T(8,128)(2,1)S(1)}, u32[]{:S(2)}, u32[]{:S(2)}) collective-permute-start(bf16[16,4096]{1,0:T(8,128)(2,1)S(1)} %get-tuple-element.47), channel_id=1, source_target_pairs={{0,192},{16,208},{32,224},{48,240},{64,0},{80,16},{96,32},{112,48}... | collective-permute-start | bytes 393224 | tf_op jit(solution)/shard_map/ppermute | solution.py:31
  194.8 5.6 %collective-permute-start.39 = (bf16[16,4096]{1,0:T(8,128)(2,1)S(1)}, bf16[16,4096]{1,0:T(8,128)(2,1)S(1)}, u32[]{:S(2)}, u32[]{:S(2)}) collective-permute-start(bf16[16,4096]{1,0:T(8,128)(2,1)S(1)} %get-tuple-element.49), channel_id=1, source_target_pairs={{0,128},{16,144},{32,160},{48,176},{64,192},{80,208},{96,224},{112... | collective-permute-start | bytes 393224 | tf_op jit(solution)/shard_map/ppermute | solution.py:31
  195.5 6.2 %collective-permute-start.40 = (bf16[16,4096]{1,0:T(8,128)(2,1)S(1)}, bf16[16,4096]{1,0:T(8,128)(2,1)S(1)}, u32[]{:S(2)}, u32[]{:S(2)}) collective-permute-start(bf16[16,4096]{1,0:T(8,128)(2,1)S(1)} %get-tuple-element.48), channel_id=1, source_target_pairs={{0,64},{16,80},{32,96},{48,112},{64,128},{80,144},{96,160},{112,17... | collective-permute-start | bytes 393224 | tf_op jit(solution)/shard_map/ppermute | solution.py:31
  195.8 6.1 %collective-permute-start.43 = (bf16[16,4096]{1,0:T(8,128)(2,1)S(1)}, bf16[16,4096]{1,0:T(8,128)(2,1)S(1)}, u32[]{:S(2)}, u32[]{:S(2)}) collective-permute-start(bf16[16,4096]{1,0:T(8,128)(2,1)S(1)} %get-tuple-element.50), channel_id=1, source_target_pairs={{0,48},{16,0},{32,16},{48,32},{64,112},{80,64},{96,80},{112,96},{1... | collective-permute-start | bytes 393224 | tf_op jit(solution)/shard_map/ppermute | solution.py:31
  195.8 6.0 %collective-permute-start.44 = (bf16[16,4096]{1,0:T(8,128)(2,1)S(1)}, bf16[16,4096]{1,0:T(8,128)(2,1)S(1)}, u32[]{:S(2)}, u32[]{:S(2)}) collective-permute-start(bf16[16,4096]{1,0:T(8,128)(2,1)S(1)} %get-tuple-element.52), channel_id=1, source_target_pairs={{0,32},{16,48},{32,0},{48,16},{64,96},{80,112},{96,64},{112,80},{1... | collective-permute-start | bytes 393224 | tf_op jit(solution)/shard_map/ppermute | solution.py:31
  197.7 5.0 %collective-permute-start.45 = (bf16[16,4096]{1,0:T(8,128)(2,1)S(1)}, bf16[16,4096]{1,0:T(8,128)(2,1)S(1)}, u32[]{:S(2)}, u32[]{:S(2)}) collective-permute-start(bf16[16,4096]{1,0:T(8,128)(2,1)S(1)} %get-tuple-element.51), channel_id=1, source_target_pairs={{0,16},{16,32},{32,48},{48,0},{64,80},{80,96},{96,112},{112,64},{1... | collective-permute-start | bytes 393224 | tf_op jit(solution)/shard_map/ppermute | solution.py:31
  203.7 26.4 %all-to-all-start.1 = ((bf16[16,2,4096]{2,1,0:T(2,128)(2,1)}), bf16[16,2,4096]{2,1,0:T(2,128)(2,1)S(1)}, u32[]{:S(2)}, u32[]{:S(2)}) async-start(bf16[16,2,4096]{2,1,0:T(2,128)(2,1)} %all_to_all.16), calls=%async_computation.1 | async-start | bytes 524288 | tf_op jit(solution)/shard_map/all_to_all | solution.py:314
